TPU v7x, 32 devices: a whole 2x2x4 slice. The times are simulated.
32 devices in a mesh: seq: 4 (over x, core), fsdp: 8 (over z, y).
Axes of the slice: x: 2, y: 2, z: 4, core: 2. Of those that a mesh axis runs over, the one named last changes fastest.
Arguments:
- inputs: bfloat16 [16, 1568, 1024], P('fsdp', 'seq'), may hold values from -7 to 7
- cotangent: bfloat16 [16, 1568, 1024], P('fsdp', 'seq'), may hold values from -6 to 6
- valid: int32 [16, 1568], P('fsdp'), may hold values from 0 to 1, as said below
- ln1_gain: bfloat16 [1024], P('fsdp'), may hold values from 0.25 to 1.75
- ln1_bias: bfloat16 [1024], P('fsdp'), may hold values from -1.75 to 1.75
- qkv_weight: bfloat16 [1024, 3072], P('fsdp'), may hold values from -0.1875 to 0.1875
- q_bias: bfloat16 [1024], P('fsdp'), may hold values from -3 to 3
- v_bias: bfloat16 [1024], P('fsdp'), may hold values from -0.3125 to 0.3125
- out_weight: bfloat16 [1024, 1024], P('fsdp'), may hold values from -2 to 2
- out_bias: bfloat16 [1024], P('fsdp'), may hold values from -1.75 to 1.75
- ln2_gain: bfloat16 [1024], P('fsdp'), may hold values from 0.25 to 1.75
- ln2_bias: bfloat16 [1024], P('fsdp'), may hold values from -1.75 to 1.75
- fc1_weight: bfloat16 [1024, 4096], P('fsdp'), may hold values from -0.1875 to 0.1875
- fc1_bias: bfloat16 [4096], P('fsdp'), may hold values from -1.75 to 1.75
- fc2_weight: bfloat16 [4096, 1024], P('fsdp'), may hold values from -0.09375 to 0.09375
- fc2_bias: bfloat16 [1024], P('fsdp'), may hold values from -1.75 to 1.75
Outputs:
- output: bfloat16 [16, 1568, 1024], P('fsdp', 'seq')
- input_grad: bfloat16 [16, 1568, 1024], P('fsdp', 'seq')
- ln1_gain_grad: float32 [1024], P('fsdp')
- ln1_bias_grad: float32 [1024], P('fsdp')
- qkv_weight_grad: float32 [1024, 3072], P('fsdp')
- q_bias_grad: float32 [1024], P('fsdp')
- v_bias_grad: float32 [1024], P('fsdp')
- out_weight_grad: float32 [1024, 1024], P('fsdp')
- out_bias_grad: float32 [1024], P('fsdp')
- ln2_gain_grad: float32 [1024], P('fsdp')
- ln2_bias_grad: float32 [1024], P('fsdp')
- fc1_weight_grad: float32 [1024, 4096], P('fsdp')
- fc1_bias_grad: float32 [4096], P('fsdp')
- fc2_weight_grad: float32 [4096, 1024], P('fsdp')
- fc2_bias_grad: float32 [1024], P('fsdp')
- branch_rms: float32 [3], replicated
Inputs may be any that keep to these rules, and one draw needn't show every extreme that they name: In every clip the valid tokens are a leading run of 392 tokens or more; some clip is valid in all its tokens.
All inputs are finite; a program needn't handle non-finite values.
Results may differ from a plain program's by a relative error of at most 0.015.
Values may be sent and summed in bfloat16 or wider, within the bound.
No kernel may reach another device: no remote copies, remote signals or barrier semaphores. Data moves between devices by JAX's collectives and lax.ppermute only.
A program may use at most 192 MiB of HBM per device.

v0:
```python
from functools import partial
import jax
import jax.numpy as jnp
from jax import lax
from jax.sharding import PartitionSpec as P

HEADS = 16
HEAD = 64
EPS = 1e-06
masked_score = -1e30


def layer_norm(values, gain, bias):
    center = values - jnp.mean(values, axis=-1, keepdims=True)
    spread = jnp.mean(center * center, axis=-1, keepdims=True)
    return center * lax.rsqrt(spread + EPS) * gain + bias


def gelu_exact(values):
    return jax.nn.gelu(values, approximate=False)


def contract_rows(left, right):
    return lax.dot_general(
        left, right, (((0,), (0,)), ((), ())), preferred_element_type=jnp.float32
    )


def times_transpose(left, right):
    return lax.dot_general(
        left, right, (((1,), (1,)), ((), ())), preferred_element_type=jnp.float32
    )


def column_sum(values):
    return jnp.sum(values, axis=0, dtype=jnp.float32)


def head_major(values, heads_here):
    clip_count, length, total_width = values.shape
    return jnp.moveaxis(values.reshape(clip_count, length, heads_here, HEAD), 2, 0)


def token_major(values):
    heads_here, clip_count, length, head_width = values.shape
    return jnp.moveaxis(values, 0, 2).reshape(clip_count, length, heads_here * head_width)


def attend_forward(pieces, keep):
    queries, key_rows, value_rows = pieces
    scores = jnp.einsum("cqd,ckd->cqk", queries, key_rows, preferred_element_type=jnp.float32)
    scores = jnp.where(keep[:, None, :], scores, masked_score)
    highest = jnp.max(scores, axis=-1, keepdims=True)
    weights = jnp.exp(scores - highest)
    totals = jnp.sum(weights, axis=-1, keepdims=True)
    probs_low = (weights / totals).astype(jnp.bfloat16)
    context = jnp.einsum(
        "cqk,ckd->cqd", probs_low, value_rows, preferred_element_type=jnp.float32
    ).astype(jnp.bfloat16)
    return (context, (highest + jnp.log(totals))[..., 0])


def attend_backward(pieces, keep):
    queries, key_rows, value_rows, log_total, grad_context = pieces
    scores = jnp.einsum("cqd,ckd->cqk", queries, key_rows, preferred_element_type=jnp.float32)
    scores = jnp.where(keep[:, None, :], scores, masked_score)
    probs = jnp.exp(scores - log_total[..., None])
    grad_probs = jnp.einsum(
        "cqd,ckd->cqk", grad_context, value_rows, preferred_element_type=jnp.float32
    )
    inner = jnp.sum(grad_probs * probs, axis=-1, keepdims=True)
    grad_scores = (probs * (grad_probs - inner)).astype(jnp.bfloat16)
    grad_queries = jnp.einsum(
        "cqk,ckd->cqd", grad_scores, key_rows, preferred_element_type=jnp.float32
    ).astype(jnp.bfloat16)
    grad_keys = jnp.einsum(
        "cqk,cqd->ckd", grad_scores, queries, preferred_element_type=jnp.float32
    ).astype(jnp.bfloat16)
    grad_values = jnp.einsum(
        "cqk,cqd->ckd", probs.astype(jnp.bfloat16), grad_context, preferred_element_type=jnp.float32
    ).astype(jnp.bfloat16)
    return (grad_queries, grad_keys, grad_values)


def body(
    inputs,
    cotangent,
    valid,
    ln1_gain,
    ln1_bias,
    qkv_weight,
    q_bias,
    v_bias,
    out_weight,
    out_bias,
    ln2_gain,
    ln2_bias,
    fc1_weight,
    fc1_bias,
    fc2_weight,
    fc2_bias,
):
    clip_count, row_count, model_width = inputs.shape
    seq_count = lax.axis_size("seq")
    heads_here = HEADS // seq_count
    scale_factor = HEAD ** (-0.5)
    shaped = (clip_count, row_count, model_width)
    key_valid = valid > 0
    full_ln1_gain, full_ln1_bias, full_qkv, full_q_bias, full_v_bias, full_out, full_out_bias = (
        lax.all_gather(ln1_gain, "fsdp", axis=0, tiled=True),
        lax.all_gather(ln1_bias, "fsdp", axis=0, tiled=True),
        lax.all_gather(qkv_weight, "fsdp", axis=0, tiled=True),
        lax.all_gather(q_bias, "fsdp", axis=0, tiled=True),
        lax.all_gather(v_bias, "fsdp", axis=0, tiled=True),
        lax.all_gather(out_weight, "fsdp", axis=0, tiled=True),
        lax.all_gather(out_bias, "fsdp", axis=0, tiled=True),
    )
    residual_in = inputs.reshape(clip_count * row_count, model_width).astype(jnp.float32)
    h_one, norm_one_pull = jax.vjp(
        layer_norm,
        residual_in,
        full_ln1_gain.astype(jnp.float32),
        full_ln1_bias.astype(jnp.float32),
    )
    h_one_low = h_one.astype(jnp.bfloat16)
    mixed = jnp.dot(h_one_low, full_qkv, preferred_element_type=jnp.float32)
    queries = ((mixed[:, :model_width] + full_q_bias.astype(jnp.float32)) * scale_factor).astype(
        jnp.bfloat16
    )
    key_rows = mixed[:, model_width : 2 * model_width].astype(jnp.bfloat16)
    value_rows = (mixed[:, 2 * model_width :] + full_v_bias.astype(jnp.float32)).astype(
        jnp.bfloat16
    )
    query_heads, key_heads, value_heads = (
        lax.all_to_all(queries.reshape(shaped), "seq", split_axis=2, concat_axis=1, tiled=True),
        lax.all_to_all(key_rows.reshape(shaped), "seq", split_axis=2, concat_axis=1, tiled=True),
        lax.all_to_all(value_rows.reshape(shaped), "seq", split_axis=2, concat_axis=1, tiled=True),
    )
    stacked = (
        head_major(query_heads, heads_here),
        head_major(key_heads, heads_here),
        head_major(value_heads, heads_here),
    )
    context_heads, log_totals = lax.map(partial(attend_forward, keep=key_valid), stacked)
    context_tokens = lax.all_to_all(
        token_major(context_heads), "seq", split_axis=1, concat_axis=2, tiled=True
    )
    context_low = context_tokens.reshape(-1, model_width)
    attn_branch = jnp.dot(
        context_low, full_out, preferred_element_type=jnp.float32
    ) + full_out_bias.astype(jnp.float32)
    residual_mid = residual_in + attn_branch
    full_ln2_gain, full_ln2_bias, full_fc1, full_fc1_bias, full_fc2, full_fc2_bias = (
        lax.all_gather(ln2_gain, "fsdp", axis=0, tiled=True),
        lax.all_gather(ln2_bias, "fsdp", axis=0, tiled=True),
        lax.all_gather(fc1_weight, "fsdp", axis=0, tiled=True),
        lax.all_gather(fc1_bias, "fsdp", axis=0, tiled=True),
        lax.all_gather(fc2_weight, "fsdp", axis=0, tiled=True),
        lax.all_gather(fc2_bias, "fsdp", axis=0, tiled=True),
    )
    h_two, norm_two_pull = jax.vjp(
        layer_norm,
        residual_mid,
        full_ln2_gain.astype(jnp.float32),
        full_ln2_bias.astype(jnp.float32),
    )
    h_two_low = h_two.astype(jnp.bfloat16)
    hidden = jnp.dot(
        h_two_low, full_fc1, preferred_element_type=jnp.float32
    ) + full_fc1_bias.astype(jnp.float32)
    active, gelu_pull = jax.vjp(gelu_exact, hidden)
    active_low = active.astype(jnp.bfloat16)
    mlp_branch = jnp.dot(
        active_low, full_fc2, preferred_element_type=jnp.float32
    ) + full_fc2_bias.astype(jnp.float32)
    residual_out = residual_mid + mlp_branch
    own_valid = (
        lax.dynamic_slice_in_dim(valid, lax.axis_index("seq") * row_count, row_count, 1)
        .reshape(-1, 1)
        .astype(jnp.float32)
    )
    totals = lax.psum(
        (
            jnp.sum(own_valid * residual_out * residual_out),
            jnp.sum(own_valid * attn_branch * attn_branch),
            jnp.sum(own_valid * mlp_branch * mlp_branch),
            jnp.sum(own_valid),
        ),
        ("seq", "fsdp"),
    )
    branch_rms = jnp.sqrt(jnp.stack([totals[0], totals[1], totals[2]]) / (totals[3] * model_width))
    full_qkv, full_out, full_fc1, full_fc2 = (
        lax.all_gather(qkv_weight, "fsdp", axis=0, tiled=True),
        lax.all_gather(out_weight, "fsdp", axis=0, tiled=True),
        lax.all_gather(fc1_weight, "fsdp", axis=0, tiled=True),
        lax.all_gather(fc2_weight, "fsdp", axis=0, tiled=True),
    )
    grad_output = cotangent.reshape(-1, model_width)
    grad_fc2_weight = contract_rows(active_low, grad_output)
    grad_fc2_bias = column_sum(grad_output)
    grad_hidden = gelu_pull(times_transpose(grad_output, full_fc2))[0].astype(jnp.bfloat16)
    grad_fc1_weight = contract_rows(h_two_low, grad_hidden)
    grad_fc1_bias = column_sum(grad_hidden)
    grad_mid, grad_ln2_gain, grad_ln2_bias = norm_two_pull(times_transpose(grad_hidden, full_fc1))
    grad_residual = grad_output.astype(jnp.float32) + grad_mid
    grad_attn = grad_residual.astype(jnp.bfloat16)
    grad_out_weight = contract_rows(context_low, grad_attn)
    grad_out_bias = column_sum(grad_attn)
    grad_context = times_transpose(grad_attn, full_out).astype(jnp.bfloat16).reshape(shaped)
    grad_context_heads = lax.all_to_all(
        grad_context, "seq", split_axis=2, concat_axis=1, tiled=True
    )
    grad_query_heads, grad_key_heads, grad_value_heads = lax.map(
        partial(attend_backward, keep=key_valid),
        stacked + (log_totals, head_major(grad_context_heads, heads_here)),
    )
    grad_queries, grad_keys, grad_values = (
        lax.all_to_all(
            token_major(grad_query_heads), "seq", split_axis=1, concat_axis=2, tiled=True
        ),
        lax.all_to_all(token_major(grad_key_heads), "seq", split_axis=1, concat_axis=2, tiled=True),
        lax.all_to_all(
            token_major(grad_value_heads), "seq", split_axis=1, concat_axis=2, tiled=True
        ),
    )
    grad_mixed = jnp.concatenate(
        [
            (grad_queries * scale_factor).reshape(-1, model_width),
            grad_keys.reshape(-1, model_width),
            grad_values.reshape(-1, model_width),
        ],
        axis=1,
    )
    grad_qkv_weight = contract_rows(h_one_low, grad_mixed)
    grad_q_bias = column_sum(grad_mixed[:, :model_width])
    grad_v_bias = column_sum(grad_mixed[:, 2 * model_width :])
    grad_first, grad_ln1_gain, grad_ln1_bias = norm_one_pull(times_transpose(grad_mixed, full_qkv))
    input_grad = (grad_residual + grad_first).astype(jnp.bfloat16).reshape(shaped)
    output = residual_out.astype(jnp.bfloat16).reshape(shaped)
    attn_part = (
        lax.psum_scatter(grad_ln1_gain, "fsdp", scatter_dimension=0, tiled=True),
        lax.psum_scatter(grad_ln1_bias, "fsdp", scatter_dimension=0, tiled=True),
        lax.psum_scatter(grad_qkv_weight, "fsdp", scatter_dimension=0, tiled=True),
        lax.psum_scatter(grad_q_bias, "fsdp", scatter_dimension=0, tiled=True),
        lax.psum_scatter(grad_v_bias, "fsdp", scatter_dimension=0, tiled=True),
        lax.psum_scatter(grad_out_weight, "fsdp", scatter_dimension=0, tiled=True),
        lax.psum_scatter(grad_out_bias, "fsdp", scatter_dimension=0, tiled=True),
    )
    mlp_part = (
        lax.psum_scatter(grad_ln2_gain, "fsdp", scatter_dimension=0, tiled=True),
        lax.psum_scatter(grad_ln2_bias, "fsdp", scatter_dimension=0, tiled=True),
        lax.psum_scatter(grad_fc1_weight, "fsdp", scatter_dimension=0, tiled=True),
        lax.psum_scatter(grad_fc1_bias, "fsdp", scatter_dimension=0, tiled=True),
        lax.psum_scatter(grad_fc2_weight, "fsdp", scatter_dimension=0, tiled=True),
        lax.psum_scatter(grad_fc2_bias, "fsdp", scatter_dimension=0, tiled=True),
    )
    shards = (
        lax.psum(attn_part[0].astype(jnp.bfloat16), "seq").astype(jnp.float32),
        lax.psum(attn_part[1].astype(jnp.bfloat16), "seq").astype(jnp.float32),
        lax.psum(attn_part[2].astype(jnp.bfloat16), "seq").astype(jnp.float32),
        lax.psum(attn_part[3].astype(jnp.bfloat16), "seq").astype(jnp.float32),
        lax.psum(attn_part[4].astype(jnp.bfloat16), "seq").astype(jnp.float32),
        lax.psum(attn_part[5].astype(jnp.bfloat16), "seq").astype(jnp.float32),
        lax.psum(attn_part[6].astype(jnp.bfloat16), "seq").astype(jnp.float32),
        lax.psum(mlp_part[0].astype(jnp.bfloat16), "seq").astype(jnp.float32),
        lax.psum(mlp_part[1].astype(jnp.bfloat16), "seq").astype(jnp.float32),
        lax.psum(mlp_part[2].astype(jnp.bfloat16), "seq").astype(jnp.float32),
        lax.psum(mlp_part[3].astype(jnp.bfloat16), "seq").astype(jnp.float32),
        lax.psum(mlp_part[4].astype(jnp.bfloat16), "seq").astype(jnp.float32),
        lax.psum(mlp_part[5].astype(jnp.bfloat16), "seq").astype(jnp.float32),
    )
    return (
        output,
        input_grad,
        shards[0],
        shards[1],
        shards[2],
        shards[3],
        shards[4],
        shards[5],
        shards[6],
        shards[7],
        shards[8],
        shards[9],
        shards[10],
        shards[11],
        shards[12],
        branch_rms,
    )


def solution(mesh):
    return jax.shard_map(
        body,
        mesh=mesh,
        in_specs=(
            P("fsdp", "seq", None),
            P("fsdp", "seq", None),
            P("fsdp", None),
            P("fsdp"),
            P("fsdp"),
            P("fsdp", None),
            P("fsdp"),
            P("fsdp"),
            P("fsdp", None),
            P("fsdp"),
            P("fsdp"),
            P("fsdp"),
            P("fsdp", None),
            P("fsdp"),
            P("fsdp", None),
            P("fsdp"),
        ),
        out_specs=(
            P("fsdp", "seq", None),
            P("fsdp", "seq", None),
            P("fsdp"),
            P("fsdp"),
            P("fsdp", None),
            P("fsdp"),
            P("fsdp"),
            P("fsdp", None),
            P("fsdp"),
            P("fsdp"),
            P("fsdp"),
            P("fsdp", None),
            P("fsdp"),
            P("fsdp", None),
            P("fsdp"),
            P(),
        ),
        check_vma=False,
    )
```

profile of v0, /device:TPU:0, one launch (start us, length us, event | category | flops | bytes accessed | tf_op | source)
XLA Modules:
  0.0 1738.8 jit_solution(8141717129016121572)
XLA Ops:
  12.0 22.4 %all-gather = bf16[8,1,128]{2,1,0:T(2,128)(2,1)S(1)} all-gather(bf16[1,1,128]{2,1,0:T(2,128)(2,1)S(1)} %bitcast.283), channel_id=1, replica_groups=mesh['seq'=4,'fsdp'=8] {'fsdp'}, dimensions={0}, use_global_device_ids=true | all-gather | bytes 2304 | tf_op jit(solution)/shard_map/all_gather | solution.py:110
  34.4 16.5 all-gather.1
  50.9 18.4 %all-gather.2 = bf16[8,1,128]{2,1,0:T(2,128)(2,1)S(1)} all-gather(bf16[1,1,128]{2,1,0:T(2,128)(2,1)S(1)} %bitcast.285), channel_id=1, replica_groups=mesh['seq'=4,'fsdp'=8] {'fsdp'}, dimensions={0}, use_global_device_ids=true | all-gather | bytes 2304 | tf_op jit(solution)/shard_map/all_gather | solution.py:113
  69.3 16.5 all-gather.3
  86.5 25.7 %all-gather.14.cloned.1.call-done = bf16[1024,3072]{1,0:T(8,128)(2,1)} async-done(((bf16[128,3072]{1,0:T(8,128)(2,1)}), bf16[1024,3072]{1,0:T(8,128)(2,1)}) %all-gather.14.cloned.1.call-update) | async-done | bytes 6291472 | tf_op jit(solution)/shard_map/all_gather | solution.py:112
  112.2 7.2 fusion.72
  131.4 6.2 copy.134
  137.6 19.5 %all-to-all-done = bf16[2,392,1024]{1,0,2:T(2,128)(2,1)S(1)} async-done(((bf16[2,392,1024]{1,0,2:T(2,128)(2,1)}), bf16[2,392,1024]{1,0,2:T(2,128)(2,1)S(1)}, u32[]{:S(2)}, u32[]{:S(2)}) %all-to-all-start) | async-done | bytes 1605664 | tf_op jit(solution)/shard_map/all_to_all | solution.py:135
  164.8 6.2 copy.131
  171.0 16.2 all-to-all-done.2
  209.5 8.0 all-to-all-done.1
  222.0 4.9 reshape.236
  229.9 58.6 %while.26 = (s32[]{:T(128)}, bf16[4,2,1568,64]{2,3,1,0:T(8,128)(2,1)}, f32[4,2,1568]{2,1,0:T(2,128)}, pred[2,1568]{1,0:T(4,128)(4,1)S(1)}, bf16[4,2,1568,64]{2,3...) while((s32[]{:T(128)}, ...), condition=%wide.region_5.6_spmd, body=%wide.region_2.5_spmd.sunk | while | flops 1303268352 | bytes 60827604 | solution.py:144
  238.2 6.4 fusion.117
  252.8 6.4 fusion.117
  267.4 6.4 fusion.117
  282.1 6.4 fusion.117
  292.5 5.5 copy.141
  301.6 18.0 %all-gather.4 = bf16[8,1,128]{2,1,0:T(2,128)(2,1)S(1)} all-gather(bf16[1,1,128]{2,1,0:T(2,128)(2,1)S(1)} %bitcast.287), channel_id=1, replica_groups=mesh['seq'=4,'fsdp'=8] {'fsdp'}, dimensions={0}, use_global_device_ids=true | all-gather | bytes 2304 | tf_op jit(solution)/shard_map/all_gather | solution.py:116
  319.7 16.5 all-gather.5
  336.2 18.3 %all-gather.6 = bf16[8,1,128]{2,1,0:T(2,128)(2,1)S(1)} all-gather(bf16[1,1,128]{2,1,0:T(2,128)(2,1)S(1)} %bitcast.289), channel_id=1, replica_groups=mesh['seq'=4,'fsdp'=8] {'fsdp'}, dimensions={0}, use_global_device_ids=true | all-gather | bytes 2304 | tf_op jit(solution)/shard_map/all_gather | solution.py:155
  354.6 26.6 %all-gather.7 = bf16[8,1,512]{2,1,0:T(2,128)(2,1)S(1)} all-gather(bf16[1,1,512]{2,1,0:T(2,128)(2,1)S(1)} %reshape.266), channel_id=1, replica_groups=mesh['seq'=4,'fsdp'=8] {'fsdp'}, dimensions={0}, use_global_device_ids=true | all-gather | bytes 9216 | tf_op jit(solution)/shard_map/all_gather | solution.py:157
  383.2 16.3 all-gather.8
  402.5 6.1 add_add_fusion.4
  410.4 13.8 fusion.67
  424.2 40.7 %convert_reduce_fusion = (f32[4096]{0:T(1024)}, bf16[784,4096]{1,0:T(8,128)(2,1)}, f32[784,4096]{1,0:T(8,128)S(1)}) fusion(f32[784,4096]{1,0:T(8,128)} %fusion.67, f32[4096]{0:T(1024)S(1)} %bitcast.262, bf16[784,1024]{1,0:T(8,128)(2,1)} %bitcast.227, bf16[4096,1024]{1,0:T(8,128)(2,1)} %all-gather.20.cloned.1.call-done), kind=kOutput, calls=%fused_computation.56 | convolution fusion | flops 6817509376 | bytes 42139648 | tf_op jit(solution)/shard_map/dot_general | solution.py:30
  469.4 11.3 fusion.73
  480.9 12.3 fusion.56
  506.6 6.3 fusion.75
  512.9 19.3 %all-to-all-done.4 = bf16[2,392,1024]{1,0,2:T(2,128)(2,1)S(1)} async-done(((bf16[2,392,1024]{1,0,2:T(2,128)(2,1)}), bf16[2,392,1024]{1,0,2:T(2,128)(2,1)S(1)}, u32[]{:S(2)}, u32[]{:S(2)}) %all-to-all-start.4) | async-done | bytes 1605664 | tf_op jit(solution)/shard_map/all_to_all | solution.py:210
  535.2 5.1 reshape.244
  544.3 235.7 %while.27 = (s32[]{:T(128)}, bf16[4,2,1568,64]{2,3,1,0:T(8,128)(2,1)}, bf16[4,2,1568,64]{2,3,1,0:T(8,128)(2,1)}, bf16[4,2,1568,64]{2,3,1,0:T(8,128)(2,1)}, pred[...) while((s32[]{:T(128)}, ...), condition=%wide.region_12.13_spmd, body=%wide.region_10.12_spmd.sunk | while | flops 3186975744 | bytes 154863216 | solution.py:213
  545.0 10.3 subtract_exponential_fusion.3
  555.3 17.3 multiply_reduce_fusion.8
  572.6 14.1 multiply_convert_fusion.3
  594.1 9.8 fusion.128
  604.6 10.1 subtract_exponential_fusion.3
  614.7 17.1 multiply_reduce_fusion.8
  631.8 13.7 multiply_convert_fusion.3
  652.9 9.6 fusion.128
  663.2 10.1 subtract_exponential_fusion.3
  673.4 17.1 multiply_reduce_fusion.8
  690.5 13.7 multiply_convert_fusion.3
  711.5 9.7 fusion.128
  721.9 10.1 subtract_exponential_fusion.3
  732.0 17.1 multiply_reduce_fusion.8
  749.2 13.7 multiply_convert_fusion.3
  770.2 9.7 fusion.128
  782.7 5.5 copy.152
  793.3 5.4 copy.156
  798.7 13.7 all-to-all-done.5
  821.8 15.4 all-to-all-done.6
  845.9 15.3 all-to-all-done.7
  865.9 9.3 fusion.74
  877.2 14.8 fusion.66
  893.4 14.7 fusion.76
  912.3 42.8 %all-reduce.9 = (f32[1]{0:T(128)}, f32[1]{0:T(128)}, f32[1]{0:T(128)}, f32[]{:T(128)}) all-reduce(f32[1]{0:T(128)} %bitcast.74, f32[1]{0:T(128)} %bitcast.73, f32[1]{0:T(128)} %bitcast.72, f32[]{:T(128)} %get-tuple-element.252), channel_id=1, replica_groups=mesh['seq'=4,'fsdp'=8] {'seq','fsdp'}, use_global_device_ids=true, to_apply=%region_56.57 | all-reduce | flops 4 | bytes 32 | tf_op jit(solution)/shard_map/psum | solution.py:182
  958.6 10.7 multiply_reduce_fusion.2
  971.0 110.5 %reduce-scatter.5.cloned.1.call-done = f32[128,3072]{1,0:T(8,128)} async-done(((f32[1024,3072]{1,0:T(8,128)}), f32[128,3072]{1,0:T(8,128)}) %reduce-scatter.5.cloned.1.call-update) | async-done | bytes 1572880 | tf_op jit(solution)/shard_map/reduce_scatter | solution.py:243
  1083.9 283.7 %reduce-scatter.9.cloned.1.call-done = f32[128,4096]{1,0:T(8,128)} async-done(((f32[1024,4096]{1,0:T(8,128)}), f32[128,4096]{1,0:T(8,128)}) %reduce-scatter.9.cloned.1.call-update) | async-done | bytes 2097168 | tf_op jit(solution)/shard_map/reduce_scatter | solution.py:252
  1370.3 283.0 %reduce-scatter.11.cloned.1.call-done = f32[512,1024]{1,0:T(8,128)} async-done(((f32[4096,1024]{1,0:T(8,128)}), f32[512,1024]{1,0:T(8,128)}) %reduce-scatter.11.cloned.1.call-update) | async-done | bytes 2097168 | tf_op jit(solution)/shard_map/reduce_scatter | solution.py:254
  1659.1 35.7 %all-reduce.10 = (bf16[1024]{0:T(1024)(128)(2,1)S(1)}, bf16[1024]{0:T(1024)(128)(2,1)S(1)}, bf16[1024]{0:T(1024)(128)(2,1)S(1)}, bf16[1024]{0:T(1024)(128)(2,1)S...) all-reduce(f32[1024]{0:T(1024)S(1)} %get-tuple-element.185, ...), channel_id=2, replica_groups=mesh['seq'=4,'fsdp'=8] {'fsdp'}, use_global_device_ids=true, to_apply=%region_16.17.clone | all-reduce | flops 12288 | bytes 73728
  1695.5 6.5 all-reduce.11
  1718.2 7.3 all-reduce.15.cloned.1.call-done
  (314 shorter events, 234.8 us)
Async XLA Ops:
  7.2 4.8 copy-start.63
  7.2 27.2 %copy-start.64 = (bf16[128]{0:T(256)(128)(2,1)S(1)}, bf16[128]{0:T(256)(128)(2,1)}, u32[]{:S(2)}) copy-start(bf16[128]{0:T(256)(128)(2,1)} %param.24) | copy-start | bytes 772
  7.2 43.6 %copy-start.65 = (bf16[128]{0:T(256)(128)(2,1)S(1)}, bf16[128]{0:T(256)(128)(2,1)}, u32[]{:S(2)}) copy-start(bf16[128]{0:T(256)(128)(2,1)} %param.26) | copy-start | bytes 772
  7.2 62.0 %copy-start.66 = (bf16[128]{0:T(256)(128)(2,1)S(1)}, bf16[128]{0:T(256)(128)(2,1)}, u32[]{:S(2)}) copy-start(bf16[128]{0:T(256)(128)(2,1)} %param.27) | copy-start | bytes 772
  7.2 104.9 %all-gather.14.cloned.1.call-start = ((), (), s32[]{:S(2)}) async-start(), calls=%async_computation.12 | async-start | bytes 7077888 | tf_op jit(solution)/shard_map/all_gather | solution.py:112
  8.0 394.5 %all-gather.16.cloned.1.call-start = ((), (), s32[]{:S(2)}) async-start(), calls=%async_computation.13 | async-start | bytes 2359296 | tf_op jit(solution)/shard_map/all_gather | solution.py:115
  8.7 400.6 %all-gather.18.cloned.1.call-start = ((), (), s32[]{:S(2)}) async-start(), calls=%async_computation.14 | async-start | bytes 9437184 | tf_op jit(solution)/shard_map/all_gather | solution.py:156
  11.3 108.1 %copy-start.30 = (f32[784]{0:T(1024)}, f32[784]{0:T(1024)S(1)}, u32[]{:S(2)}) copy-start(f32[784]{0:T(1024)S(1)} %div.53) | copy-start | bytes 9412
  11.9 73.8 %copy-start.43 = (f32[784]{0:T(1024)}, f32[784]{0:T(1024)S(1)}, u32[]{:S(2)}) copy-start(f32[784]{0:T(1024)S(1)} %add.176) | copy-start | bytes 9412
  11.9 73.8 %copy-start.32 = (f32[784]{0:T(1024)}, f32[784]{0:T(1024)S(1)}, u32[]{:S(2)}) copy-start(f32[784]{0:T(1024)S(1)} %rsqrt.20) | copy-start | bytes 9412
  34.4 51.4 %copy-start.34 = (f32[8,1,128]{2,1,0:T(1,128)}, f32[8,1,128]{2,1,0:T(1,128)S(1)}, u32[]{:S(2)}) copy-start(f32[8,1,128]{2,1,0:T(1,128)S(1)} %convert_element_type.259) | copy-start | bytes 12292
  86.4 33.0 %copy-start.23 = (bf16[784,1024]{1,0:T(8,128)(2,1)}, bf16[784,1024]{1,0:T(8,128)(2,1)S(1)}, u32[]{:S(2)}) copy-start(bf16[784,1024]{1,0:T(8,128)(2,1)S(1)} %add_convert_fusion.3) | copy-start | bytes 4816900
  119.4 4.3 copy-start.18
  127.7 29.3 %all-to-all-start = ((bf16[2,392,1024]{1,0,2:T(2,128)(2,1)}), bf16[2,392,1024]{1,0,2:T(2,128)(2,1)S(1)}, u32[]{:S(2)}, u32[]{:S(2)}) async-start(bf16[2,392,1024]{1,0,2:T(2,128)(2,1)} %copy.128), calls=%async_computation | async-start | bytes 4194304 | tf_op jit(solution)/shard_map/all_to_all | solution.py:135
  157.0 30.2 %all-to-all-start.2 = ((bf16[2,392,1024]{1,0,2:T(2,128)(2,1)}), bf16[2,392,1024]{1,0,2:T(2,128)(2,1)}, u32[]{:S(2)}, u32[]{:S(2)}) async-start(bf16[2,392,1024]{1,0,2:T(2,128)(2,1)} %copy.134), calls=%async_computation.2 | async-start | bytes 4194304 | tf_op jit(solution)/shard_map/all_to_all | solution.py:137
  171.0 21.3 %copy-start.45 = (s32[2,1568]{1,0:T(2,128)S(1)}, s32[2,1568]{1,0:T(2,128)}, u32[]{:S(2)}) copy-start(s32[2,1568]{1,0:T(2,128)} %param.22) | copy-start | bytes 37636
  187.3 30.2 %all-to-all-start.1 = ((bf16[2,392,1024]{1,0,2:T(2,128)(2,1)}), bf16[2,392,1024]{1,0,2:T(2,128)(2,1)}, u32[]{:S(2)}, u32[]{:S(2)}) async-start(bf16[2,392,1024]{1,0,2:T(2,128)(2,1)} %copy.131), calls=%async_computation.1 | async-start | bytes 4194304 | tf_op jit(solution)/shard_map/all_to_all | solution.py:136
  191.7 232.5 %all-gather.20.cloned.1.call-start = ((), (), s32[]{:S(2)}) async-start(), calls=%async_computation.15 | async-start | bytes 9437184 | tf_op jit(solution)/shard_map/all_gather | solution.py:158
  288.5 9.6 copy-start
  288.5 9.6 copy-start.21
  288.5 114.0 %copy-start.2 = (bf16[4,2,1568,64]{2,3,1,0:T(8,128)(2,1)}, bf16[4,2,1568,64]{2,3,1,0:T(8,128)(2,1)S(1)}, u32[]{:S(2)}) copy-start(bf16[4,2,1568,64]{2,3,1,0:T(8,128)(2,1)S(1)} %get-tuple-element.457) | copy-start | bytes 4816900
  292.5 9.1 copy-start.67
  292.5 27.2 %copy-start.68 = (bf16[128]{0:T(256)(128)(2,1)S(1)}, bf16[128]{0:T(256)(128)(2,1)}, u32[]{:S(2)}) copy-start(bf16[128]{0:T(256)(128)(2,1)} %param.30) | copy-start | bytes 772
  292.5 43.8 %copy-start.69 = (bf16[128]{0:T(256)(128)(2,1)S(1)}, bf16[128]{0:T(256)(128)(2,1)}, u32[]{:S(2)}) copy-start(bf16[128]{0:T(256)(128)(2,1)} %param.31) | copy-start | bytes 772
  292.5 62.0 %copy-start.62 = (bf16[512]{0:T(512)(128)(2,1)S(1)}, bf16[512]{0:T(512)(128)(2,1)}, u32[]{:S(2)}) copy-start(bf16[512]{0:T(512)(128)(2,1)} %param.33) | copy-start | bytes 3076
  292.5 90.7 %copy-start.70 = (bf16[128]{0:T(256)(128)(2,1)S(1)}, bf16[128]{0:T(256)(128)(2,1)}, u32[]{:S(2)}) copy-start(bf16[128]{0:T(256)(128)(2,1)} %param.35) | copy-start | bytes 772
  298.1 102.0 %all-to-all-start.3 = ((bf16[2,1568,256]{2,0,1:T(2,128)(2,1)}), bf16[2,1568,256]{2,0,1:T(2,128)(2,1)S(1)}, u32[]{:S(2)}, u32[]{:S(2)}) async-start(bf16[2,1568,256]{2,0,1:T(2,128)(2,1)} %copy.141), calls=%async_computation.3 | async-start | bytes 3211264 | tf_op jit(solution)/shard_map/all_to_all | solution.py:145
  319.7 82.8 %copy-start.58 = (f32[8,1,128]{2,1,0:T(1,128)}, f32[8,1,128]{2,1,0:T(1,128)S(1)}, u32[]{:S(2)}) copy-start(f32[8,1,128]{2,1,0:T(1,128)S(1)} %convert_element_type.263) | copy-start | bytes 12292
  336.2 73.1 %copy-start.47 = (f32[8,1,128]{2,1,0:T(1,128)}, f32[8,1,128]{2,1,0:T(1,128)S(1)}, u32[]{:S(2)}) copy-start(f32[8,1,128]{2,1,0:T(1,128)S(1)} %convert_element_type.264) | copy-start | bytes 12292
  354.5 54.8 %copy-start.56 = (f32[8,1,128]{2,1,0:T(1,128)}, f32[8,1,128]{2,1,0:T(1,128)S(1)}, u32[]{:S(2)}) copy-start(f32[8,1,128]{2,1,0:T(1,128)S(1)} %convert_element_type.265) | copy-start | bytes 12292
  408.8 15.4 copy-start.38
  409.3 14.9 copy-start.41
  409.3 14.9 copy-start.50
  424.2 40.7 %copy-start.16 = (f32[784,4096]{1,0:T(8,128)S(1)}, f32[784,4096]{1,0:T(8,128)}, u32[]{:S(2)}) copy-start(f32[784,4096]{1,0:T(8,128)} %fusion.67) | copy-start | bytes 38535172
  464.9 15.8 slice-start
  469.4 11.4 copy-start.6
  469.4 11.4 copy-start.19
  469.4 11.4 copy-start.39
  469.4 11.4 copy-start.48
  469.4 11.4 copy-start.51
  469.4 11.4 copy-start.59
  469.4 11.4 copy-start.60
  469.4 11.4 copy-start.61
  469.4 11.4 slice-start.1
  480.8 12.3 copy-start.42
  503.0 29.3 %all-to-all-start.4 = ((bf16[2,392,1024]{1,0,2:T(2,128)(2,1)}), bf16[2,392,1024]{1,0,2:T(2,128)(2,1)S(1)}, u32[]{:S(2)}, u32[]{:S(2)}) async-start(bf16[2,392,1024]{1,0,2:T(2,128)(2,1)} %copy.144), calls=%async_computation.4 | async-start | bytes 4194304 | tf_op jit(solution)/shard_map/all_to_all | solution.py:210
  506.6 462.7 %reduce-scatter.7.cloned.1.call-start = ((), (), s32[]{:S(2)}) async-start(), calls=%async_computation.17 | async-start | bytes 4718592 | tf_op jit(solution)/shard_map/reduce_scatter | solution.py:246
  782.7 9.3 copy-start.17
  788.2 24.2 %all-to-all-start.5 = ((bf16[2,1568,256]{2,0,1:T(2,128)(2,1)}), bf16[2,1568,256]{2,0,1:T(2,128)(2,1)S(1)}, u32[]{:S(2)}, u32[]{:S(2)}) async-start(bf16[2,1568,256]{2,0,1:T(2,128)(2,1)} %copy.152), calls=%async_computation.5 | async-start | bytes 3211264 | tf_op jit(solution)/shard_map/all_to_all | solution.py:218
  812.4 28.5 %copy-start.10 = (bf16[2,1568,256]{2,0,1:T(2,128)(2,1)}, bf16[2,1568,256]{2,0,1:T(2,128)(2,1)S(1)}, u32[]{:S(2)}) copy-start(bf16[2,1568,256]{2,0,1:T(2,128)(2,1)S(1)} %all-to-all-done.5) | copy-start | bytes 4816900
  812.4 24.9 %all-to-all-start.6 = ((bf16[2,1568,256]{2,0,1:T(2,128)(2,1)}), bf16[2,1568,256]{2,0,1:T(2,128)(2,1)}, u32[]{:S(2)}, u32[]{:S(2)}) async-start(bf16[2,1568,256]{2,0,1:T(2,128)(2,1)} %copy.156), calls=%async_computation.6 | async-start | bytes 3211264 | tf_op jit(solution)/shard_map/all_to_all | solution.py:221
  837.2 24.0 %all-to-all-start.7 = ((bf16[2,1568,256]{2,0,1:T(2,128)(2,1)}), bf16[2,1568,256]{2,0,1:T(2,128)(2,1)S(1)}, u32[]{:S(2)}, u32[]{:S(2)}) async-start(bf16[2,1568,256]{2,0,1:T(2,128)(2,1)} %copy.160), calls=%async_computation.7 | async-start | bytes 3211264 | tf_op jit(solution)/shard_map/all_to_all | solution.py:222
  840.8 240.7 %reduce-scatter.5.cloned.1.call-start = ((), (), s32[]{:S(2)}) async-start(), calls=%async_computation.16 | async-start | bytes 14155776 | tf_op jit(solution)/shard_map/reduce_scatter | solution.py:243
  875.3 492.3 %reduce-scatter.9.cloned.1.call-start = ((), (), s32[]{:S(2)}) async-start(), calls=%async_computation.18 | async-start | bytes 18874368 | tf_op jit(solution)/shard_map/reduce_scatter | solution.py:252
  892.0 761.3 %reduce-scatter.11.cloned.1.call-start = ((), (), s32[]{:S(2)}) async-start(), calls=%async_computation.19 | async-start | bytes 18874368 | tf_op jit(solution)/shard_map/reduce_scatter | solution.py:254
  908.1 50.2 %copy-start.13 = (bf16[2,1568,256]{2,1,0:T(8,128)(2,1)S(1)}, bf16[2,1568,256]{2,1,0:T(8,128)(2,1)}, u32[]{:S(2)}) copy-start(bf16[2,1568,256]{2,1,0:T(8,128)(2,1)} %copy-done.12) | copy-start | bytes 4816900
  908.1 50.4 %copy-start.9 = (bf16[2,392,1024]{2,1,0:T(8,128)(2,1)S(1)}, bf16[2,392,1024]{2,1,0:T(8,128)(2,1)}, u32[]{:S(2)}) copy-start(bf16[2,392,1024]{2,1,0:T(8,128)(2,1)} %param.20) | copy-start | bytes 4816900
  908.1 50.4 %copy-start.31 = (f32[784]{0:T(1024)S(1)}, f32[784]{0:T(1024)}, u32[]{:S(2)}) copy-start(f32[784]{0:T(1024)} %copy-done.30) | copy-start | bytes 9412
  908.1 50.4 %copy-start.33 = (f32[784]{0:T(1024)S(1)}, f32[784]{0:T(1024)}, u32[]{:S(2)}) copy-start(f32[784]{0:T(1024)} %copy-done.32) | copy-start | bytes 9412
  908.1 50.4 %copy-start.35 = (f32[8,1,128]{2,1,0:T(1,128)S(1)}, f32[8,1,128]{2,1,0:T(1,128)}, u32[]{:S(2)}) copy-start(f32[8,1,128]{2,1,0:T(1,128)} %copy-done.34) | copy-start | bytes 12292
  908.1 817.3 %all-reduce.15.cloned.1.call-start = ((), (), s32[]{:S(2)}) async-start(), calls=%async_computation.20 | async-start | bytes 6291456 | tf_op jit(solution)/shard_map/psum | solution.py:260
  1370.3 285.7 %copy-start.11 = (bf16[2,1568,256]{2,0,1:T(2,128)(2,1)S(1)}, bf16[2,1568,256]{2,0,1:T(2,128)(2,1)}, u32[]{:S(2)}) copy-start(bf16[2,1568,256]{2,0,1:T(2,128)(2,1)} %copy-done.10) | copy-start | bytes 4816900
  1656.0 50.6 %copy-start.44 = (f32[784]{0:T(1024)S(1)}, f32[784]{0:T(1024)}, u32[]{:S(2)}) copy-start(f32[784]{0:T(1024)} %copy-done.43) | copy-start | bytes 9412
  1725.5 4.5 copy-start.27
  (28 other events, 67.1 us)
Sparse Core Ops, SparseCore 0:
  10.2 101.8 all-gather.13
  114.3 47.4 all-gather.15
  164.0 123.4 all-gather.17
  289.4 123.5 all-gather.19
  513.0 87.4 reduce-scatter.6
  875.4 206.0 reduce-scatter.4
  1085.8 281.7 reduce-scatter.8
  1371.4 281.8 reduce-scatter.10
  1657.2 68.2 all-reduce.14
where the time goes:
time: 1750 us; the launch traced here: 1740 us
  waiting for transfers between devices  820 us (47%)
  matrix products  365 us (21%)
  blocking collectives  254 us (15%)
  other arithmetic  130 us (7%)
  local copies, waits for them, and re-layouts  120 us (7%)
  starting transfers between devices  32.3 us (2%)
    reduce_scatter x1, waiting for transfers between devices, body(): lax.psum_scatter(grad_fc1_weight, 'fsdp', scatter_dimension=0, tiled=True)  284 us
    reduce_scatter x1, waiting for transfers between devices, body(): lax.psum_scatter(grad_fc2_weight, 'fsdp', scatter_dimension=0, tiled=True)  283 us
    reduce_scatter x1, waiting for transfers between devices, body(): lax.psum_scatter(grad_qkv_weight, 'fsdp', scatter_dimension=0, tiled=True)  110 us
    dot_general x4, matrix products, attend_backward(): jnp.einsum('cqd,ckd->cqk', grad_context, value_rows, preferred_element_ty...  68.7 us
    dot_general x4, matrix products, times_transpose(): lax.dot_general(left, right, (((1,), (1,)), ((), ())), preferred_element_...  64.5 us
    convert_element_type x4, other arithmetic, attend_backward(): grad_scores = (probs * (grad_probs - inner)).astype(jnp.bfloat16)  55.1 us
    dot_general x4, matrix products, contract_rows(): lax.dot_general(left, right, (((0,), (0,)), ((), ())), preferred_element_...  45.1 us
    psum x1, blocking collectives, body(): lax.psum((jnp.sum(own_valid * residual_out * residual_out), jnp.sum(own_v...  42.8 us
  transfers between devices with their start and end apart: 17, of which 12 were waited for; matrix products, arithmetic and copies ran while one was open for 30% of the time, Pallas kernels for 0%

commit v1 on v0

--- a/solution.py
+++ b/solution.py
@@ -3,6 +3,7 @@
 import jax.numpy as jnp
 from jax import lax
 from jax.sharding import PartitionSpec as P
+from jax.lax import psum
 
 HEADS = 16
 HEAD = 64
@@ -179,15 +180,13 @@
         .reshape(-1, 1)
         .astype(jnp.float32)
     )
-    totals = lax.psum(
-        (
-            jnp.sum(own_valid * residual_out * residual_out),
-            jnp.sum(own_valid * attn_branch * attn_branch),
-            jnp.sum(own_valid * mlp_branch * mlp_branch),
-            jnp.sum(own_valid),
-        ),
-        ("seq", "fsdp"),
-    )
+    field_in = (
+        jnp.sum(own_valid * residual_out * residual_out),
+        jnp.sum(own_valid * attn_branch * attn_branch),
+        jnp.sum(own_valid * mlp_branch * mlp_branch),
+        jnp.sum(own_valid),
+    )
+    totals = psum(psum(field_in, axis_name="seq"), "fsdp")
     branch_rms = jnp.sqrt(jnp.stack([totals[0], totals[1], totals[2]]) / (totals[3] * model_width))
     full_qkv, full_out, full_fc1, full_fc2 = (
         lax.all_gather(qkv_weight, "fsdp", axis=0, tiled=True),

time: 1750 us -> 1750 us (level)
  blocking collectives: 254 us -> 218 us
  waiting for transfers between devices: 820 us -> 856 us
    reduce_scatter x1, waiting for transfers between devices: 110 us -> 148 us  [body(): lax.psum_scatter(grad_qkv_weight, 'fsdp', scatter_dimension=0, tiled=True)]
    psum x1, blocking collectives: 42.8 us -> 6.71 us  [body(): totals = psum(psum(field_in, axis_name='seq'), 'fsdp')]
where the time goes in v1:
time: 1750 us; the launch traced here: 1740 us
  waiting for transfers between devices  856 us (49%)
  matrix products  365 us (21%)
  blocking collectives  218 us (12%)
  other arithmetic  130 us (7%)
  local copies, waits for them, and re-layouts  120 us (7%)
  starting transfers between devices  32.2 us (2%)
    reduce_scatter x1, waiting for transfers between devices, body(): lax.psum_scatter(grad_fc1_weight, 'fsdp', scatter_dimension=0, tiled=True)  284 us
    reduce_scatter x1, waiting for transfers between devices, body(): lax.psum_scatter(grad_fc2_weight, 'fsdp', scatter_dimension=0, tiled=True)  283 us
    reduce_scatter x1, waiting for transfers between devices, body(): lax.psum_scatter(grad_qkv_weight, 'fsdp', scatter_dimension=0, tiled=True)  148 us
    dot_general x4, matrix products, attend_backward(): jnp.einsum('cqd,ckd->cqk', grad_context, value_rows, preferred_element_ty...  68.7 us
    dot_general x4, matrix products, times_transpose(): lax.dot_general(left, right, (((1,), (1,)), ((), ())), preferred_element_...  64.5 us
    convert_element_type x4, other arithmetic, attend_backward(): grad_scores = (probs * (grad_probs - inner)).astype(jnp.bfloat16)  55.1 us
    dot_general x4, matrix products, contract_rows(): lax.dot_general(left, right, (((0,), (0,)), ((), ())), preferred_element_...  44.9 us
    dot_general x4, matrix products, attend_backward(): jnp.einsum('cqd,ckd->cqk', queries, key_rows, preferred_element_type=jnp....  40.7 us
  transfers between devices with their start and end apart: 17, of which 12 were waited for; matrix products, arithmetic and copies ran while one was open for 30% of the time, Pallas kernels for 0%

profile of v1, /device:TPU:0, one launch (start us, length us, event | category | flops | bytes accessed | tf_op | source)
XLA Modules:
  0.0 1738.0 jit_solution(11855731812495855105)
XLA Ops:
  12.0 22.4 %all-gather = bf16[8,1,128]{2,1,0:T(2,128)(2,1)S(1)} all-gather(bf16[1,1,128]{2,1,0:T(2,128)(2,1)S(1)} %bitcast.283), channel_id=1, replica_groups=mesh['seq'=4,'fsdp'=8] {'fsdp'}, dimensions={0}, use_global_device_ids=true | all-gather | bytes 2304 | tf_op jit(solution)/shard_map/all_gather | solution.py:111
  34.4 16.5 all-gather.1
  50.9 18.4 %all-gather.2 = bf16[8,1,128]{2,1,0:T(2,128)(2,1)S(1)} all-gather(bf16[1,1,128]{2,1,0:T(2,128)(2,1)S(1)} %bitcast.285), channel_id=1, replica_groups=mesh['seq'=4,'fsdp'=8] {'fsdp'}, dimensions={0}, use_global_device_ids=true | all-gather | bytes 2304 | tf_op jit(solution)/shard_map/all_gather | solution.py:114
  69.3 16.5 all-gather.3
  86.5 25.7 %all-gather.14.cloned.1.call-done = bf16[1024,3072]{1,0:T(8,128)(2,1)} async-done(((bf16[128,3072]{1,0:T(8,128)(2,1)}), bf16[1024,3072]{1,0:T(8,128)(2,1)}) %all-gather.14.cloned.1.call-update) | async-done | bytes 6291472 | tf_op jit(solution)/shard_map/all_gather | solution.py:113
  112.2 7.2 fusion.72
  131.4 6.2 copy.134
  137.6 19.5 %all-to-all-done = bf16[2,392,1024]{1,0,2:T(2,128)(2,1)S(1)} async-done(((bf16[2,392,1024]{1,0,2:T(2,128)(2,1)}), bf16[2,392,1024]{1,0,2:T(2,128)(2,1)S(1)}, u32[]{:S(2)}, u32[]{:S(2)}) %all-to-all-start) | async-done | bytes 1605664 | tf_op jit(solution)/shard_map/all_to_all | solution.py:136
  164.8 6.2 copy.131
  171.0 16.2 all-to-all-done.2
  209.4 8.1 all-to-all-done.1
  222.0 4.9 reshape.236
  229.9 58.6 %while.26 = (s32[]{:T(128)}, bf16[4,2,1568,64]{2,3,1,0:T(8,128)(2,1)}, f32[4,2,1568]{2,1,0:T(2,128)}, pred[2,1568]{1,0:T(4,128)(4,1)S(1)}, bf16[4,2,1568,64]{2,3...) while((s32[]{:T(128)}, ...), condition=%wide.region_5.6_spmd, body=%wide.region_2.5_spmd.sunk | while | flops 1303268352 | bytes 60827604 | solution.py:145
  238.2 6.4 fusion.117
  252.8 6.4 fusion.117
  267.4 6.4 fusion.117
  282.1 6.4 fusion.117
  292.5 5.5 copy.141
  301.7 18.0 %all-gather.4 = bf16[8,1,128]{2,1,0:T(2,128)(2,1)S(1)} all-gather(bf16[1,1,128]{2,1,0:T(2,128)(2,1)S(1)} %bitcast.287), channel_id=1, replica_groups=mesh['seq'=4,'fsdp'=8] {'fsdp'}, dimensions={0}, use_global_device_ids=true | all-gather | bytes 2304 | tf_op jit(solution)/shard_map/all_gather | solution.py:117
  319.7 16.5 all-gather.5
  336.2 18.3 %all-gather.6 = bf16[8,1,128]{2,1,0:T(2,128)(2,1)S(1)} all-gather(bf16[1,1,128]{2,1,0:T(2,128)(2,1)S(1)} %bitcast.289), channel_id=1, replica_groups=mesh['seq'=4,'fsdp'=8] {'fsdp'}, dimensions={0}, use_global_device_ids=true | all-gather | bytes 2304 | tf_op jit(solution)/shard_map/all_gather | solution.py:156
  354.6 26.6 %all-gather.7 = bf16[8,1,512]{2,1,0:T(2,128)(2,1)S(1)} all-gather(bf16[1,1,512]{2,1,0:T(2,128)(2,1)S(1)} %reshape.266), channel_id=1, replica_groups=mesh['seq'=4,'fsdp'=8] {'fsdp'}, dimensions={0}, use_global_device_ids=true | all-gather | bytes 9216 | tf_op jit(solution)/shard_map/all_gather | solution.py:158
  383.2 16.3 all-gather.8
  402.4 6.1 add_add_fusion.4
  410.4 13.8 fusion.67
  424.2 40.7 %convert_reduce_fusion = (f32[4096]{0:T(1024)}, bf16[784,4096]{1,0:T(8,128)(2,1)}, f32[784,4096]{1,0:T(8,128)S(1)}) fusion(f32[784,4096]{1,0:T(8,128)} %fusion.67, f32[4096]{0:T(1024)S(1)} %bitcast.262, bf16[784,1024]{1,0:T(8,128)(2,1)} %bitcast.227, bf16[4096,1024]{1,0:T(8,128)(2,1)} %all-gather.20.cloned.1.call-done), kind=kOutput, calls=%fused_computation.56 | convolution fusion | flops 6817509376 | bytes 42139648 | tf_op jit(solution)/shard_map/dot_general | solution.py:31
  469.4 11.3 fusion.73
  480.8 12.3 fusion.56
  506.6 6.3 fusion.75
  512.9 19.3 %all-to-all-done.4 = bf16[2,392,1024]{1,0,2:T(2,128)(2,1)S(1)} async-done(((bf16[2,392,1024]{1,0,2:T(2,128)(2,1)}), bf16[2,392,1024]{1,0,2:T(2,128)(2,1)S(1)}, u32[]{:S(2)}, u32[]{:S(2)}) %all-to-all-start.4) | async-done | bytes 1605664 | tf_op jit(solution)/shard_map/all_to_all | solution.py:209
  535.1 5.1 reshape.244
  544.2 235.7 %while.27 = (s32[]{:T(128)}, bf16[4,2,1568,64]{2,3,1,0:T(8,128)(2,1)}, bf16[4,2,1568,64]{2,3,1,0:T(8,128)(2,1)}, bf16[4,2,1568,64]{2,3,1,0:T(8,128)(2,1)}, pred[...) while((s32[]{:T(128)}, ...), condition=%wide.region_12.13_spmd, body=%wide.region_10.12_spmd.sunk | while | flops 3186975744 | bytes 154863216 | solution.py:212
  545.0 10.3 subtract_exponential_fusion.3
  555.3 17.3 multiply_reduce_fusion.8
  572.6 14.1 multiply_convert_fusion.3
  594.1 9.8 fusion.128
  604.6 10.1 subtract_exponential_fusion.3
  614.7 17.1 multiply_reduce_fusion.8
  631.8 13.7 multiply_convert_fusion.3
  652.9 9.6 fusion.128
  663.2 10.1 subtract_exponential_fusion.3
  673.3 17.1 multiply_reduce_fusion.8
  690.5 13.7 multiply_convert_fusion.3
  711.5 9.7 fusion.128
  721.9 10.1 subtract_exponential_fusion.3
  732.0 17.1 multiply_reduce_fusion.8
  749.2 13.7 multiply_convert_fusion.3
  770.2 9.7 fusion.128
  782.7 5.5 copy.152
  793.3 5.4 copy.156
  798.7 13.7 all-to-all-done.5
  821.8 15.4 all-to-all-done.6
  845.9 15.3 all-to-all-done.7
  865.9 9.3 fusion.74
  877.1 14.8 fusion.66
  893.4 14.6 fusion.76
  912.2 6.7 all-reduce.10
  920.5 10.7 multiply_reduce_fusion.2
  932.9 147.7 %reduce-scatter.5.cloned.1.call-done = f32[128,3072]{1,0:T(8,128)} async-done(((f32[1024,3072]{1,0:T(8,128)}), f32[128,3072]{1,0:T(8,128)}) %reduce-scatter.5.cloned.1.call-update) | async-done | bytes 1572880 | tf_op jit(solution)/shard_map/reduce_scatter | solution.py:242
  1083.1 283.7 %reduce-scatter.9.cloned.1.call-done = f32[128,4096]{1,0:T(8,128)} async-done(((f32[1024,4096]{1,0:T(8,128)}), f32[128,4096]{1,0:T(8,128)}) %reduce-scatter.9.cloned.1.call-update) | async-done | bytes 2097168 | tf_op jit(solution)/shard_map/reduce_scatter | solution.py:251
  1369.5 282.8 %reduce-scatter.11.cloned.1.call-done = f32[512,1024]{1,0:T(8,128)} async-done(((f32[4096,1024]{1,0:T(8,128)}), f32[512,1024]{1,0:T(8,128)}) %reduce-scatter.11.cloned.1.call-update) | async-done | bytes 2097168 | tf_op jit(solution)/shard_map/reduce_scatter | solution.py:253
  1656.8 35.8 %all-reduce.9 = (bf16[1024]{0:T(1024)(128)(2,1)S(1)}, bf16[1024]{0:T(1024)(128)(2,1)S(1)}, bf16[1024]{0:T(1024)(128)(2,1)S(1)}, bf16[1024]{0:T(1024)(128)(2,1)S(...) all-reduce(f32[1024]{0:T(1024)S(1)} %get-tuple-element.185, ...), channel_id=2, replica_groups=mesh['seq'=4,'fsdp'=8] {'fsdp'}, use_global_device_ids=true, to_apply=%region_16.17.clone | all-reduce | flops 12292 | bytes 73760
  1693.3 5.7 all-reduce.11
  1717.8 6.6 all-reduce.15.cloned.1.call-done
  (314 shorter events, 234.2 us)
Async XLA Ops:
  7.2 4.8 copy-start.63
  7.2 27.2 %copy-start.64 = (bf16[128]{0:T(256)(128)(2,1)S(1)}, bf16[128]{0:T(256)(128)(2,1)}, u32[]{:S(2)}) copy-start(bf16[128]{0:T(256)(128)(2,1)} %param.24) | copy-start | bytes 772
  7.2 43.6 %copy-start.65 = (bf16[128]{0:T(256)(128)(2,1)S(1)}, bf16[128]{0:T(256)(128)(2,1)}, u32[]{:S(2)}) copy-start(bf16[128]{0:T(256)(128)(2,1)} %param.26) | copy-start | bytes 772
  7.2 62.0 %copy-start.66 = (bf16[128]{0:T(256)(128)(2,1)S(1)}, bf16[128]{0:T(256)(128)(2,1)}, u32[]{:S(2)}) copy-start(bf16[128]{0:T(256)(128)(2,1)} %param.27) | copy-start | bytes 772
  7.2 104.9 %all-gather.14.cloned.1.call-start = ((), (), s32[]{:S(2)}) async-start(), calls=%async_computation.12 | async-start | bytes 7077888 | tf_op jit(solution)/shard_map/all_gather | solution.py:113
  8.0 394.5 %all-gather.16.cloned.1.call-start = ((), (), s32[]{:S(2)}) async-start(), calls=%async_computation.13 | async-start | bytes 2359296 | tf_op jit(solution)/shard_map/all_gather | solution.py:116
  8.7 400.6 %all-gather.18.cloned.1.call-start = ((), (), s32[]{:S(2)}) async-start(), calls=%async_computation.14 | async-start | bytes 9437184 | tf_op jit(solution)/shard_map/all_gather | solution.py:157
  11.3 108.1 %copy-start.30 = (f32[784]{0:T(1024)}, f32[784]{0:T(1024)S(1)}, u32[]{:S(2)}) copy-start(f32[784]{0:T(1024)S(1)} %div.53) | copy-start | bytes 9412
  11.9 73.8 %copy-start.43 = (f32[784]{0:T(1024)}, f32[784]{0:T(1024)S(1)}, u32[]{:S(2)}) copy-start(f32[784]{0:T(1024)S(1)} %add.184) | copy-start | bytes 9412
  11.9 73.8 %copy-start.32 = (f32[784]{0:T(1024)}, f32[784]{0:T(1024)S(1)}, u32[]{:S(2)}) copy-start(f32[784]{0:T(1024)S(1)} %rsqrt.20) | copy-start | bytes 9412
  34.4 51.4 %copy-start.34 = (f32[8,1,128]{2,1,0:T(1,128)}, f32[8,1,128]{2,1,0:T(1,128)S(1)}, u32[]{:S(2)}) copy-start(f32[8,1,128]{2,1,0:T(1,128)S(1)} %convert_element_type.259) | copy-start | bytes 12292
  86.4 33.0 %copy-start.23 = (bf16[784,1024]{1,0:T(8,128)(2,1)}, bf16[784,1024]{1,0:T(8,128)(2,1)S(1)}, u32[]{:S(2)}) copy-start(bf16[784,1024]{1,0:T(8,128)(2,1)S(1)} %add_convert_fusion.3) | copy-start | bytes 4816900
  127.8 29.3 %all-to-all-start = ((bf16[2,392,1024]{1,0,2:T(2,128)(2,1)}), bf16[2,392,1024]{1,0,2:T(2,128)(2,1)S(1)}, u32[]{:S(2)}, u32[]{:S(2)}) async-start(bf16[2,392,1024]{1,0,2:T(2,128)(2,1)} %copy.128), calls=%async_computation | async-start | bytes 4194304 | tf_op jit(solution)/shard_map/all_to_all | solution.py:136
  157.0 30.2 %all-to-all-start.2 = ((bf16[2,392,1024]{1,0,2:T(2,128)(2,1)}), bf16[2,392,1024]{1,0,2:T(2,128)(2,1)}, u32[]{:S(2)}, u32[]{:S(2)}) async-start(bf16[2,392,1024]{1,0,2:T(2,128)(2,1)} %copy.134), calls=%async_computation.2 | async-start | bytes 4194304 | tf_op jit(solution)/shard_map/all_to_all | solution.py:138
  171.0 21.3 %copy-start.45 = (s32[2,1568]{1,0:T(2,128)S(1)}, s32[2,1568]{1,0:T(2,128)}, u32[]{:S(2)}) copy-start(s32[2,1568]{1,0:T(2,128)} %param.22) | copy-start | bytes 37636
  187.3 30.2 %all-to-all-start.1 = ((bf16[2,392,1024]{1,0,2:T(2,128)(2,1)}), bf16[2,392,1024]{1,0,2:T(2,128)(2,1)}, u32[]{:S(2)}, u32[]{:S(2)}) async-start(bf16[2,392,1024]{1,0,2:T(2,128)(2,1)} %copy.131), calls=%async_computation.1 | async-start | bytes 4194304 | tf_op jit(solution)/shard_map/all_to_all | solution.py:137
  191.7 232.4 %all-gather.20.cloned.1.call-start = ((), (), s32[]{:S(2)}) async-start(), calls=%async_computation.15 | async-start | bytes 9437184 | tf_op jit(solution)/shard_map/all_gather | solution.py:159
  288.5 9.6 copy-start
  288.5 9.6 copy-start.21
  288.5 113.9 %copy-start.2 = (bf16[4,2,1568,64]{2,3,1,0:T(8,128)(2,1)}, bf16[4,2,1568,64]{2,3,1,0:T(8,128)(2,1)S(1)}, u32[]{:S(2)}) copy-start(bf16[4,2,1568,64]{2,3,1,0:T(8,128)(2,1)S(1)} %get-tuple-element.461) | copy-start | bytes 4816900
  292.5 9.1 copy-start.67
  292.5 27.2 %copy-start.68 = (bf16[128]{0:T(256)(128)(2,1)S(1)}, bf16[128]{0:T(256)(128)(2,1)}, u32[]{:S(2)}) copy-start(bf16[128]{0:T(256)(128)(2,1)} %param.30) | copy-start | bytes 772
  292.5 43.7 %copy-start.69 = (bf16[128]{0:T(256)(128)(2,1)S(1)}, bf16[128]{0:T(256)(128)(2,1)}, u32[]{:S(2)}) copy-start(bf16[128]{0:T(256)(128)(2,1)} %param.31) | copy-start | bytes 772
  292.5 62.0 %copy-start.62 = (bf16[512]{0:T(512)(128)(2,1)S(1)}, bf16[512]{0:T(512)(128)(2,1)}, u32[]{:S(2)}) copy-start(bf16[512]{0:T(512)(128)(2,1)} %param.33) | copy-start | bytes 3076
  292.5 90.7 %copy-start.70 = (bf16[128]{0:T(256)(128)(2,1)S(1)}, bf16[128]{0:T(256)(128)(2,1)}, u32[]{:S(2)}) copy-start(bf16[128]{0:T(256)(128)(2,1)} %param.35) | copy-start | bytes 772
  298.1 102.0 %all-to-all-start.3 = ((bf16[2,1568,256]{2,0,1:T(2,128)(2,1)}), bf16[2,1568,256]{2,0,1:T(2,128)(2,1)S(1)}, u32[]{:S(2)}, u32[]{:S(2)}) async-start(bf16[2,1568,256]{2,0,1:T(2,128)(2,1)} %copy.141), calls=%async_computation.3 | async-start | bytes 3211264 | tf_op jit(solution)/shard_map/all_to_all | solution.py:146
  319.7 82.7 %copy-start.58 = (f32[8,1,128]{2,1,0:T(1,128)}, f32[8,1,128]{2,1,0:T(1,128)S(1)}, u32[]{:S(2)}) copy-start(f32[8,1,128]{2,1,0:T(1,128)S(1)} %convert_element_type.263) | copy-start | bytes 12292
  336.2 73.1 %copy-start.47 = (f32[8,1,128]{2,1,0:T(1,128)}, f32[8,1,128]{2,1,0:T(1,128)S(1)}, u32[]{:S(2)}) copy-start(f32[8,1,128]{2,1,0:T(1,128)S(1)} %convert_element_type.264) | copy-start | bytes 12292
  354.5 54.8 %copy-start.56 = (f32[8,1,128]{2,1,0:T(1,128)}, f32[8,1,128]{2,1,0:T(1,128)S(1)}, u32[]{:S(2)}) copy-start(f32[8,1,128]{2,1,0:T(1,128)S(1)} %convert_element_type.265) | copy-start | bytes 12292
  408.8 15.4 copy-start.38
  409.2 14.9 copy-start.41
  409.3 14.9 copy-start.50
  424.2 40.7 %copy-start.16 = (f32[784,4096]{1,0:T(8,128)S(1)}, f32[784,4096]{1,0:T(8,128)}, u32[]{:S(2)}) copy-start(f32[784,4096]{1,0:T(8,128)} %fusion.67) | copy-start | bytes 38535172
  464.9 15.8 slice-start
  469.3 11.4 copy-start.6
  469.3 11.4 copy-start.19
  469.3 11.4 copy-start.39
  469.3 11.4 copy-start.48
  469.3 11.4 copy-start.51
  469.4 11.4 copy-start.59
  469.4 11.4 copy-start.60
  469.4 11.4 copy-start.61
  469.4 11.4 slice-start.1
  480.8 12.3 copy-start.42
  502.9 29.3 %all-to-all-start.4 = ((bf16[2,392,1024]{1,0,2:T(2,128)(2,1)}), bf16[2,392,1024]{1,0,2:T(2,128)(2,1)S(1)}, u32[]{:S(2)}, u32[]{:S(2)}) async-start(bf16[2,392,1024]{1,0,2:T(2,128)(2,1)} %copy.144), calls=%async_computation.4 | async-start | bytes 4194304 | tf_op jit(solution)/shard_map/all_to_all | solution.py:209
  506.5 424.6 %reduce-scatter.7.cloned.1.call-start = ((), (), s32[]{:S(2)}) async-start(), calls=%async_computation.17 | async-start | bytes 4718592 | tf_op jit(solution)/shard_map/reduce_scatter | solution.py:245
  782.7 9.3 copy-start.17
  788.2 24.2 %all-to-all-start.5 = ((bf16[2,1568,256]{2,0,1:T(2,128)(2,1)}), bf16[2,1568,256]{2,0,1:T(2,128)(2,1)S(1)}, u32[]{:S(2)}, u32[]{:S(2)}) async-start(bf16[2,1568,256]{2,0,1:T(2,128)(2,1)} %copy.152), calls=%async_computation.5 | async-start | bytes 3211264 | tf_op jit(solution)/shard_map/all_to_all | solution.py:217
  812.4 28.5 %copy-start.10 = (bf16[2,1568,256]{2,0,1:T(2,128)(2,1)}, bf16[2,1568,256]{2,0,1:T(2,128)(2,1)S(1)}, u32[]{:S(2)}) copy-start(bf16[2,1568,256]{2,0,1:T(2,128)(2,1)S(1)} %all-to-all-done.5) | copy-start | bytes 4816900
  812.4 24.9 %all-to-all-start.6 = ((bf16[2,1568,256]{2,0,1:T(2,128)(2,1)}), bf16[2,1568,256]{2,0,1:T(2,128)(2,1)}, u32[]{:S(2)}, u32[]{:S(2)}) async-start(bf16[2,1568,256]{2,0,1:T(2,128)(2,1)} %copy.156), calls=%async_computation.6 | async-start | bytes 3211264 | tf_op jit(solution)/shard_map/all_to_all | solution.py:220
  837.2 24.0 %all-to-all-start.7 = ((bf16[2,1568,256]{2,0,1:T(2,128)(2,1)}), bf16[2,1568,256]{2,0,1:T(2,128)(2,1)S(1)}, u32[]{:S(2)}, u32[]{:S(2)}) async-start(bf16[2,1568,256]{2,0,1:T(2,128)(2,1)} %copy.160), calls=%async_computation.7 | async-start | bytes 3211264 | tf_op jit(solution)/shard_map/all_to_all | solution.py:221
  840.8 239.9 %reduce-scatter.5.cloned.1.call-start = ((), (), s32[]{:S(2)}) async-start(), calls=%async_computation.16 | async-start | bytes 14155776 | tf_op jit(solution)/shard_map/reduce_scatter | solution.py:242
  875.3 491.5 %reduce-scatter.9.cloned.1.call-start = ((), (), s32[]{:S(2)}) async-start(), calls=%async_computation.18 | async-start | bytes 18874368 | tf_op jit(solution)/shard_map/reduce_scatter | solution.py:251
  892.0 760.3 %reduce-scatter.11.cloned.1.call-start = ((), (), s32[]{:S(2)}) async-start(), calls=%async_computation.19 | async-start | bytes 18874368 | tf_op jit(solution)/shard_map/reduce_scatter | solution.py:253
  907.9 11.0 copy-start.11
  907.9 12.5 copy-start.9
  908.0 12.5 copy-start.31
  908.0 12.5 copy-start.33
  908.0 12.5 copy-start.35
  908.0 816.4 %all-reduce.15.cloned.1.call-start = ((), (), s32[]{:S(2)}) async-start(), calls=%async_computation.20 | async-start | bytes 6291456 | tf_op jit(solution)/shard_map/psum | solution.py:259
  1369.5 285.5 %copy-start.13 = (bf16[2,1568,256]{2,1,0:T(8,128)(2,1)S(1)}, bf16[2,1568,256]{2,1,0:T(8,128)(2,1)}, u32[]{:S(2)}) copy-start(bf16[2,1568,256]{2,1,0:T(8,128)(2,1)} %copy-done.12) | copy-start | bytes 4816900
  1655.0 48.8 %copy-start.44 = (f32[784]{0:T(1024)S(1)}, f32[784]{0:T(1024)}, u32[]{:S(2)}) copy-start(f32[784]{0:T(1024)} %copy-done.43) | copy-start | bytes 9412
  1708.2 5.4 copy-start.4
  1708.2 5.4 copy-start.37
  (28 other events, 64.8 us)
Sparse Core Ops, SparseCore 0:
  10.2 101.8 all-gather.13
  114.3 47.4 all-gather.15
  164.0 123.4 all-gather.17
  289.4 123.5 all-gather.19
  513.0 87.3 reduce-scatter.6
  875.4 205.2 reduce-scatter.4
  1084.9 281.7 reduce-scatter.8
  1370.6 281.6 reduce-scatter.10
  1656.2 68.1 all-reduce.14
